TPU v7x, 256 devices: a whole 4x4x8 slice. The times are simulated.
256 devices in a mesh: rep: 4 (over y), ep: 64 (over z, x, core).
Axes of the slice: x: 4, y: 4, z: 8, core: 2. Of those that a mesh axis runs over, the one named last changes fastest.
Arguments:
- tokens: bfloat16 [8192, 4096], P(('rep', 'ep')), parts along dimension 0, may hold values from -170 to 170
- norm_gain: float32 [4096], replicated, may hold values from 0.1 to 1.9
- gate_weight: bfloat16 [256, 4096, 768], P(('rep', 'ep')), parts along dimension 0, may hold values from -0.09375 to 0.09375
- up_weight: bfloat16 [256, 4096, 768], P(('rep', 'ep')), parts along dimension 0, may hold values from -0.09375 to 0.09375
- route_ids: int32 [8192, 8], P(('rep', 'ep')), parts along dimension 0, may hold values from 0 to 63, all different within a row; in each aligned block of 32 rows (0 to 31, 32 to 63, ...) at most 8 rows name the same one
- route_scores: float32 [8192, 8], P(('rep', 'ep')), parts along dimension 0, may hold values from 0.1 to 1
- queries: bfloat16 [8192, 4096], P(('rep', 'ep')), parts along dimension 0, may hold values from -500 to 500
- key_cache: bfloat16 [8192, 16, 256], P(('rep', 'ep')), parts along dimension 0, may hold values from -7 to 7
- value_cache: bfloat16 [8192, 16, 256], P(('rep', 'ep')), parts along dimension 0, may hold values from -6 to 6
- new_keys: bfloat16 [8192, 256], P(('rep', 'ep')), parts along dimension 0, may hold values from -6 to 6
- new_values: bfloat16 [8192, 256], P(('rep', 'ep')), parts along dimension 0, may hold values from -6 to 6
- cache_lengths: int32 [8192], P(('rep', 'ep')), parts along dimension 0, may hold values from 2 to 16, as said below
Outputs:
- expert_terms: bfloat16 [8192, 8, 768], P(('rep', 'ep')), parts along dimension 0
- attended: bfloat16 [8192, 4096], P(('rep', 'ep')), parts along dimension 0
There are 4 independent parts, one for each index of `rep`. A program takes and returns all parts, laid end to end along the dimension named above; an argument that names none is the same for every part. Nothing has to cross between parts.
Inputs may be any that keep to these rules, and one draw needn't show every extreme that they name: `route_ids`: each row names 8 different experts; among the rows of one device no expert is named more than 8 times, a bound that some block reaches. `cache_lengths`: some row has exactly 16.
All inputs are finite; a program needn't handle non-finite values.
Results may differ from a plain program's by a relative error of at most 0.02.
Values may be sent and summed in bfloat16 or wider, within the bound.
A program may use at most 128 MiB of HBM per device.

v0:
```python
import jax
import jax.numpy as jnp
from jax import lax
from jax.sharding import PartitionSpec as P

HD = 128


def rms_rows(hidden, norm_gain):
    values = hidden.astype(jnp.float32)
    mean_sq = jnp.mean(values * values, axis=-1, keepdims=True)
    return (values * lax.rsqrt(mean_sq + 1e-06) * norm_gain).astype(jnp.bfloat16)


def expert_apply(buffer, gate_mat, up_mat):
    gate_val = jnp.einsum("nsd,df->nsf", buffer, gate_mat, preferred_element_type=jnp.float32)
    up_val = jnp.einsum("nsd,df->nsf", buffer, up_mat, preferred_element_type=jnp.float32)
    return (jax.nn.silu(gate_val) * up_val).astype(jnp.bfloat16)


def attend_rows(queries, key_cache, value_cache, new_keys, new_values, cache_lengths):
    row_count = key_cache.shape[0]
    cache_len = key_cache.shape[1]
    kv_heads = new_keys.shape[1] // HD
    group_size = queries.shape[1] // new_keys.shape[1]
    query_heads = queries.reshape(row_count, kv_heads, group_size, HD)
    key_heads = key_cache.reshape(row_count, cache_len, kv_heads, HD)
    value_heads = value_cache.reshape(row_count, cache_len, kv_heads, HD)
    factor = HD ** (-0.5)
    scores = (
        jnp.einsum("tkgd,tckd->tkgc", query_heads, key_heads, preferred_element_type=jnp.float32)
        * factor
    )
    own_score = (
        jnp.einsum(
            "tkgd,tkd->tkg",
            query_heads,
            new_keys.reshape(row_count, kv_heads, HD),
            preferred_element_type=jnp.float32,
        )
        * factor
    )
    live_mask = (jnp.arange(cache_len, dtype=jnp.int32)[None, :] < cache_lengths[:, None])[
        :, None, None, :
    ]
    scores = jnp.where(live_mask, scores, -1e30)
    top_score = jnp.maximum(jnp.max(scores, axis=-1), own_score)
    weights = jnp.where(live_mask, jnp.exp(scores - top_score[..., None]), 0.0)
    own_weight = jnp.exp(own_score - top_score)
    total_mass = jnp.sum(weights, axis=-1) + own_weight
    prob_bf = (weights / total_mass[..., None]).astype(jnp.bfloat16)
    own_prob = (own_weight / total_mass).astype(jnp.bfloat16)
    attn_sum = jnp.einsum(
        "tkgc,tckd->tkgd", prob_bf, value_heads, preferred_element_type=jnp.float32
    )
    fresh = new_values.astype(jnp.float32).reshape(row_count, kv_heads, 1, HD)
    attn_sum = attn_sum + own_prob.astype(jnp.float32)[..., None] * fresh
    return attn_sum.reshape(row_count, -1).astype(jnp.bfloat16)


def local(
    tokens,
    norm_gain,
    gate_weight,
    up_weight,
    route_ids,
    route_scores,
    queries,
    key_cache,
    value_cache,
    new_keys,
    new_values,
    cache_lengths,
):
    attended = attend_rows(queries, key_cache, value_cache, new_keys, new_values, cache_lengths)
    hidden = (tokens.astype(jnp.float32) + attended.astype(jnp.float32)).astype(jnp.bfloat16)
    normed = rms_rows(hidden, norm_gain)
    experts = lax.axis_size("ep")
    tok_count = route_ids.shape[0]
    top_count = route_ids.shape[1]
    capacity = min(tok_count, 2 * tok_count * top_count // experts)
    expert_ids = jnp.arange(experts, dtype=jnp.int32)
    slot_ids = jnp.arange(capacity, dtype=jnp.int32)
    route_hot = route_ids[:, :, None] == expert_ids[None, None, :]
    hit_mask = jnp.any(route_hot, axis=1).astype(jnp.int32)
    slot_rank = jnp.cumsum(hit_mask, axis=0) - hit_mask
    row_slot = jnp.sum(jnp.where(route_hot, slot_rank[:, None, :], 0), axis=2)
    gate_mat = gate_weight[0]
    up_mat = up_weight[0]
    placing = (
        (hit_mask.T[:, None, :] == 1) & (slot_rank.T[:, None, :] == slot_ids[None, :, None])
    ).astype(jnp.bfloat16)
    outgoing = jnp.einsum(
        "est,td->esd", placing, normed, preferred_element_type=jnp.float32
    ).astype(jnp.bfloat16)
    received = expert_apply(
        lax.all_to_all(outgoing, "ep", split_axis=0, concat_axis=0, tiled=True),
        gate_mat=gate_mat,
        up_mat=up_mat,
    )
    returned = lax.all_to_all(received, "ep", split_axis=0, concat_axis=0, tiled=True)
    pick_map = (
        route_hot[:, :, :, None] & (row_slot[:, :, None, None] == slot_ids[None, None, None, :])
    ).astype(jnp.bfloat16)
    picked = jnp.einsum("tkes,esf->tkf", pick_map, returned, preferred_element_type=jnp.float32)
    route_share = route_scores / jnp.sum(route_scores, axis=1, keepdims=True)
    expert_terms = (route_share[:, :, None] * picked).astype(jnp.bfloat16)
    return (expert_terms, attended)


def solution(mesh):
    return jax.shard_map(
        local,
        mesh=mesh,
        in_specs=(
            P(("rep", "ep"), None),
            P(),
            P(("rep", "ep"), None, None),
            P(("rep", "ep"), None, None),
            P(("rep", "ep"), None),
            P(("rep", "ep"), None),
            P(("rep", "ep"), None),
            P(("rep", "ep"), None, None),
            P(("rep", "ep"), None, None),
            P(("rep", "ep"), None),
            P(("rep", "ep"), None),
            P(("rep", "ep")),
        ),
        out_specs=(P(("rep", "ep"), None, None), P(("rep", "ep"), None)),
        check_vma=False,
    )
```

profile of v0, /device:TPU:1, one launch (start us, length us, event | category | flops | bytes accessed | tf_op | source)
XLA Modules:
  0.0 155.4 jit_solution(5067827590854339085)
XLA Ops:
  0.7 0.8 iota_compare_fusion.3
  1.5 1.0 copy.28
  2.5 0.7 reshape.85
  3.2 0.2 fusion.40
  3.4 1.3 fusion.39
  4.7 0.2 fusion.18
  5.0 0.1 fusion.38
  5.0 0.7 reshape.76
  5.8 0.5 fusion.9
  6.3 0.2 fusion.13
  6.6 0.1 copy.15
  6.7 0.1 iota_compare_fusion.2
  6.8 0.1 reduce_window_sum.11
  6.9 0.1 copy.17
  7.0 0.1 copy.16
  7.1 1.3 convolution_convert_fusion
  8.4 107.7 %all_to_all.10 = bf16[64,8,4096]{2,1,0:T(8,128)(2,1)S(1)} all-to-all(bf16[64,8,4096]{2,1,0:T(8,128)(2,1)S(1)} %convolution_convert_fusion), channel_id=1, replica_groups=mesh['rep'=4,'ep'=64] {'ep'}, dimensions={0} | all-to-all | bytes 8388608 | tf_op jit(solution)/shard_map/all_to_all | solution.py:97
  116.1 3.5 %fusion.2 = f32[64,8,768]{2,1,0:T(8,128)S(1)} fusion(bf16[64,8,4096]{2,1,0:T(8,128)(2,1)S(1)} %all_to_all.10, bf16[1,4096,768]{2,1,0:T(8,128)(2,1)S(1)} %bitcast.65), kind=kOutput, calls=%fused_computation.2 | convolution fusion | flops 3221225472 | bytes 12058624 | tf_op jit(solution)/shard_map/nsd,df->nsf/dot_general | solution.py:16
  119.6 4.5 %multiply_convert_fusion = bf16[64,8,768]{2,1,0:T(8,128)(2,1)} fusion(f32[64,8,768]{2,1,0:T(8,128)S(1)} %fusion.2, bf16[64,8,4096]{2,1,0:T(8,128)(2,1)S(1)} %all_to_all.10, bf16[1,4096,768]{2,1,0:T(8,128)(2,1)S(1)} %bitcast.67), kind=kOutput, calls=%fused_computation.5 | convolution fusion | flops 3223584768 | bytes 12845056 | tf_op jit(solution)/shard_map/nsd,df->nsf/dot_general | solution.py:17
  124.1 7.0 %all-to-all-start.1 = ((bf16[64,8,768]{2,1,0:T(8,128)(2,1)}), bf16[64,8,768]{2,1,0:T(8,128)(2,1)S(1)}, u32[]{:S(2)}, u32[]{:S(2)}) async-start(bf16[64,8,768]{2,1,0:T(8,128)(2,1)} %multiply_convert_fusion), calls=%async_computation.1 | async-start | bytes 1572864 | tf_op jit(solution)/shard_map/all_to_all | solution.py:101
  131.1 0.1 copy.14
  131.2 0.7 select_reduce_fusion
  131.9 21.9 %all-to-all-done.1 = bf16[64,8,768]{2,1,0:T(8,128)(2,1)S(1)} async-done(((bf16[64,8,768]{2,1,0:T(8,128)(2,1)}), bf16[64,8,768]{2,1,0:T(8,128)(2,1)S(1)}, u32[]{:S(2)}, u32[]{:S(2)}) %all-to-all-start.1) | async-done | bytes 786464 | tf_op jit(solution)/shard_map/all_to_all | solution.py:101
  153.8 1.5 fusion.7
  (29 shorter events, 0.2 us)
Async XLA Ops:
  0.6 5.1 %copy-start = (bf16[32,16,256]{2,1,0:T(8,128)(2,1)S(1)}, bf16[32,16,256]{2,1,0:T(8,128)(2,1)}, u32[]{:S(2)}) copy-start(bf16[32,16,256]{2,1,0:T(8,128)(2,1)} %param.20) | copy-start | bytes 786436
  0.6 5.7 %copy-start.1 = (bf16[32,4096]{1,0:T(8,128)(2,1)S(1)}, bf16[32,4096]{1,0:T(8,128)(2,1)}, u32[]{:S(2)}) copy-start(bf16[32,4096]{1,0:T(8,128)(2,1)} %param.12) | copy-start | bytes 786436
  0.7 5.9 %copy-start.5 = (s32[32,8]{0,1:T(8,128)S(1)}, s32[32,8]{0,1:T(8,128)}, u32[]{:S(2)}) copy-start(s32[32,8]{0,1:T(8,128)} %param.16) | copy-start | bytes 3076
  0.7 6.4 %copy-start.3 = (f32[4096]{0:T(1024)S(1)}, f32[4096]{0:T(1024)}, u32[]{:S(2)}) copy-start(f32[4096]{0:T(1024)} %param.13) | copy-start | bytes 49156
  6.6 109.5 %copy-start.2 = (bf16[32,4096]{1,0:T(8,128)(2,1)}, bf16[32,4096]{1,0:T(8,128)(2,1)S(1)}, u32[]{:S(2)}) copy-start(bf16[32,4096]{1,0:T(8,128)(2,1)S(1)} %get-tuple-element.3) | copy-start | bytes 786436
  7.1 109.0 %slice-start = ((s8[6291456]{0:T(1024)(128)(4,1)}), s8[4194304]{0:T(1024)(128)(4,1)S(1)}, s32[]{:S(2)}) async-start(s8[6291456]{0:T(1024)(128)(4,1)} %bitcast.64), calls=%async_computation.2 | async-start | bytes 8388608
  8.4 107.7 %slice-start.1 = ((s8[6291456]{0:T(1024)(128)(4,1)}), s8[2097152]{0:T(1024)(128)(4,1)S(1)}, s32[]{:S(2)}) async-start(s8[6291456]{0:T(1024)(128)(4,1)} %bitcast.64), calls=%async_computation.3 | async-start | bytes 4194304
  8.4 111.2 %slice-start.2 = ((s8[6291456]{0:T(1024)(128)(4,1)}), s8[4194304]{0:T(1024)(128)(4,1)S(1)}, s32[]{:S(2)}) async-start(s8[6291456]{0:T(1024)(128)(4,1)} %bitcast.66), calls=%async_computation.4 | async-start | bytes 8388608
  116.1 3.5 %slice-start.3 = ((s8[6291456]{0:T(1024)(128)(4,1)}), s8[2097152]{0:T(1024)(128)(4,1)S(1)}, s32[]{:S(2)}) async-start(s8[6291456]{0:T(1024)(128)(4,1)} %bitcast.66), calls=%async_computation.5 | async-start | bytes 4194304
  119.6 11.5 %copy-start.4 = (f32[32,8]{0,1:T(8,128)S(1)}, f32[32,8]{0,1:T(8,128)}, u32[]{:S(2)}) copy-start(f32[32,8]{0,1:T(8,128)} %param.17) | copy-start | bytes 3076
  124.1 29.8 %all-to-all-start.1 = ((bf16[64,8,768]{2,1,0:T(8,128)(2,1)}), bf16[64,8,768]{2,1,0:T(8,128)(2,1)S(1)}, u32[]{:S(2)}, u32[]{:S(2)}) async-start(bf16[64,8,768]{2,1,0:T(8,128)(2,1)} %multiply_convert_fusion), calls=%async_computation.1 | async-start | bytes 1572864 | tf_op jit(solution)/shard_map/all_to_all | solution.py:101
where the time goes:
time: 156 us; the launch traced here: 155 us
  blocking collectives  108 us (69%)
  waiting for transfers between devices  21.9 us (14%)
  matrix products  12.7 us (8%)
  starting transfers between devices  7.02 us (4%)
  local copies, waits for them, and re-layouts  2.86 us (2%)
  other arithmetic  2.28 us (1%)
    all_to_all x1, blocking collectives, local(): lax.all_to_all(outgoing, 'ep', split_axis=0, concat_axis=0, tiled=True)  108 us
    all_to_all x1, waiting for transfers between devices, local(): lax.all_to_all(received, 'ep', split_axis=0, concat_axis=0, tiled=True)  21.9 us
    all_to_all x1, starting transfers between devices, local(): lax.all_to_all(received, 'ep', split_axis=0, concat_axis=0, tiled=True)  7.02 us
    dot_general x1, matrix products, expert_apply(): jnp.einsum('nsd,df->nsf', buffer, up_mat, preferred_element_type=jnp.floa...  4.45 us
    dot_general x1, matrix products, expert_apply(): jnp.einsum('nsd,df->nsf', buffer, gate_mat, preferred_element_type=jnp.fl...  3.46 us
  transfers between devices with their start and end apart: 1, of which 1 were waited for; matrix products, arithmetic and copies ran while one was open for 1% of the time, Pallas kernels for 0%

commit v1 on v0

--- a/solution.py
+++ b/solution.py
@@ -1,21 +1,26 @@
 import jax
+import jax.experimental.pallas as pl
+import jax.experimental.pallas.tpu as pltpu
 import jax.numpy as jnp
 from jax import lax
 from jax.sharding import PartitionSpec as P
 
 HD = 128
+D = 4096
+FFW = 768
+TOK = 32
+CAP = 8
+NZ = 8
+PLANE = 8
+META = 128
+HALF = D // 2
+MESH = pl.DeviceIdType.MESH
 
 
 def rms_rows(hidden, norm_gain):
     values = hidden.astype(jnp.float32)
     mean_sq = jnp.mean(values * values, axis=-1, keepdims=True)
     return (values * lax.rsqrt(mean_sq + 1e-06) * norm_gain).astype(jnp.bfloat16)
-
-
-def expert_apply(buffer, gate_mat, up_mat):
-    gate_val = jnp.einsum("nsd,df->nsf", buffer, gate_mat, preferred_element_type=jnp.float32)
-    up_val = jnp.einsum("nsd,df->nsf", buffer, up_mat, preferred_element_type=jnp.float32)
-    return (jax.nn.silu(gate_val) * up_val).astype(jnp.bfloat16)
 
 
 def attend_rows(queries, key_cache, value_cache, new_keys, new_values, cache_lengths):
@@ -58,6 +63,312 @@
     return attn_sum.reshape(row_count, -1).astype(jnp.bfloat16)
 
 
+def layer_kernel(
+    rows_ref, gate_hbm, up_hbm, pos_ref, share_ref, out_ref,
+    raw, half_out, pair_out, half_in, pair_in, gate_w, up_w, act, ret_out, ret_in,
+    w_sem, z_send, z_recv, p_send, p_recv, r_send, r_recv,
+):
+    ep = lax.axis_index("ep")
+    z = ep // PLANE
+    spot = ep % PLANE
+
+    def at_z(dz):
+        return (z + dz + NZ) % NZ
+
+    def dev(zz, ss):
+        return {"ep": zz * PLANE + ss}
+
+    w_copies = [
+        pltpu.make_async_copy(gate_hbm.at[0], gate_w, w_sem.at[0]),
+        pltpu.make_async_copy(up_hbm.at[0], up_w, w_sem.at[1]),
+    ]
+    for copy in w_copies:
+        copy.start()
+    barrier = pltpu.get_barrier_semaphore()
+
+    def greet(o, carry):
+        pl.semaphore_signal(
+            barrier, inc=1, device_id={"ep": (ep + o) % (NZ * PLANE)}, device_id_type=MESH
+        )
+        return carry
+
+    lax.fori_loop(1, NZ * PLANE, greet, 0)
+    raw[z] = rows_ref[...]
+    pl.semaphore_wait(barrier, NZ * PLANE - 1)
+
+    def hop(sign, k):
+        block = raw.at[at_z(-sign * (k - 1))]
+        if k == 4:
+            block = block.at[pl.ds(0 if sign > 0 else 16, 16)]
+        idx = (k - 1) + (0 if sign > 0 else 4)
+        return pltpu.make_async_remote_copy(
+            src_ref=block,
+            dst_ref=block,
+            send_sem=z_send.at[idx],
+            recv_sem=z_recv.at[idx],
+            device_id=dev(at_z(sign), spot),
+            device_id_type=MESH,
+        )
+
+    def arrived(sign, k):
+        block = raw.at[at_z(-sign * k)]
+        if k == 4:
+            block = block.at[pl.ds(0 if sign > 0 else 16, 16)]
+        idx = (k - 1) + (0 if sign > 0 else 4)
+        pltpu.make_async_remote_copy(
+            src_ref=block,
+            dst_ref=block,
+            send_sem=z_send.at[idx],
+            recv_sem=z_recv.at[idx],
+            device_id=dev(at_z(sign), spot),
+            device_id_type=MESH,
+        ).wait_recv()
+
+    slot_row = lax.broadcasted_iota(jnp.int32, (PLANE * CAP, META), 0)
+    lane = lax.broadcasted_iota(jnp.int32, (PLANE * CAP, META), 1)
+    expert_hot = (lane == z * PLANE + slot_row // CAP).astype(jnp.bfloat16)
+    wanted = (
+        lax.broadcasted_iota(jnp.int32, (PLANE * CAP, TOK), 0) % CAP
+    ).astype(jnp.float32)
+
+    def placing(zz):
+        meta = raw[zz, :, D:]
+        ranks = lax.dot_general(
+            expert_hot, meta, (((1,), (1,)), ((), ())), preferred_element_type=jnp.float32
+        )
+        return (ranks == wanted).astype(jnp.float32).astype(jnp.bfloat16)
+
+    def slots(place, zz, lo, width):
+        got = jnp.dot(place, raw[zz, :, lo : lo + width], preferred_element_type=jnp.float32)
+        return got.reshape(PLANE, CAP, width)
+
+    def compact_half(i, zz):
+        place = placing(zz)
+        for lo in range(0, HALF, 1024):
+            both = jnp.concatenate(
+                [slots(place, zz, lo, 1024), slots(place, zz, HALF + lo, 1024)], axis=1
+            )
+            half_out[i, :, :, lo : lo + 1024] = both.astype(jnp.bfloat16)
+
+    def compact_pair(k):
+        upper, lower = at_z(k), at_z(-k)
+        place_u, place_l = placing(upper), placing(lower)
+        for lo in range(0, D, 1024):
+            both = jnp.concatenate(
+                [slots(place_u, upper, lo, 1024), slots(place_l, lower, lo, 1024)], axis=1
+            )
+            pair_out[k - 1, :, :, lo : lo + 1024] = both.astype(jnp.bfloat16)
+
+    def plane_refs(chunk):
+        if chunk in (0, 4):
+            return half_out.at[chunk // 4], half_in.at[chunk // 4]
+        return pair_out.at[chunk - 1], pair_in.at[chunk - 1]
+
+    def plane_copy(chunk, o):
+        outgoing, incoming = plane_refs(chunk)
+        target = (spot + o) % PLANE
+        return pltpu.make_async_remote_copy(
+            src_ref=outgoing.at[target],
+            dst_ref=incoming.at[spot],
+            send_sem=p_send.at[chunk * PLANE + target],
+            recv_sem=p_recv.at[chunk * PLANE + spot],
+            device_id=dev(z, target),
+            device_id_type=MESH,
+        )
+
+    def plane_own(chunk):
+        outgoing, incoming = plane_refs(chunk)
+        return pltpu.make_async_copy(
+            outgoing.at[spot], incoming.at[spot], p_recv.at[chunk * PLANE + spot]
+        )
+
+    def plane_start(chunk):
+        for o in range(1, PLANE):
+            plane_copy(chunk, o).start()
+        plane_own(chunk).start()
+
+    def plane_wait(chunk):
+        outgoing, incoming = plane_refs(chunk)
+        for o in range(1, PLANE):
+            source = (spot + o) % PLANE
+            pltpu.make_async_remote_copy(
+                src_ref=outgoing.at[source],
+                dst_ref=incoming.at[source],
+                send_sem=p_send.at[chunk * PLANE + source],
+                recv_sem=p_recv.at[chunk * PLANE + source],
+                device_id=dev(z, source),
+                device_id_type=MESH,
+            ).wait_recv()
+        plane_own(chunk).wait()
+
+    def gated(gate_val, up_val):
+        return gate_val / (1.0 + jnp.exp(-gate_val)) * up_val
+
+    def give_back(values, dz_index):
+        both = jnp.concatenate([values[:, :, : FFW // 2], values[:, :, FFW // 2 :]], axis=1)
+        ret_out[dz_index] = both.astype(jnp.bfloat16)
+
+    def ret_copy(dz, r):
+        idx = (dz + NZ) % NZ
+        return pltpu.make_async_remote_copy(
+            src_ref=ret_out.at[idx, r],
+            dst_ref=ret_in.at[ep],
+            send_sem=r_send.at[idx * PLANE + r],
+            recv_sem=r_recv.at[ep],
+            device_id=dev(at_z(dz), r),
+            device_id_type=MESH,
+        )
+
+    def ret_own():
+        return pltpu.make_async_copy(ret_out.at[0, spot], ret_in.at[ep], r_recv.at[ep])
+
+    def ret_start(dz):
+        for o in range(PLANE):
+            if dz == 0 and o == 0:
+                ret_own().start()
+            else:
+                ret_copy(dz, (spot + o) % PLANE).start()
+
+    def expert_half(chunk):
+        plane_wait(chunk)
+        for lo in range(0, FFW, 256):
+            rows = half_in[chunk // 4].reshape(PLANE * 16, HALF)
+
+            def halves(mat):
+                first = jnp.dot(
+                    rows, mat[:HALF, lo : lo + 256], preferred_element_type=jnp.float32
+                ).reshape(PLANE, 16, 256)
+                second = jnp.dot(
+                    rows, mat[HALF:, lo : lo + 256], preferred_element_type=jnp.float32
+                ).reshape(PLANE, 16, 256)
+                return first[:, :CAP] + second[:, CAP:]
+
+            act[:, :CAP, lo : lo + 256] = gated(halves(gate_w), halves(up_w))
+        give_back(act[:, :CAP], chunk)
+        ret_start(chunk)
+
+    def expert_pair(k):
+        plane_wait(k)
+        for lo in range(0, FFW, 256):
+            rows = pair_in[k - 1].reshape(PLANE * 16, D)
+            gate_val = jnp.dot(rows, gate_w[:, lo : lo + 256], preferred_element_type=jnp.float32)
+            up_val = jnp.dot(rows, up_w[:, lo : lo + 256], preferred_element_type=jnp.float32)
+            act[:, :, lo : lo + 256] = gated(gate_val, up_val).reshape(PLANE, 16, 256)
+        give_back(act[:, :CAP], k)
+        give_back(act[:, CAP:], NZ - k)
+        ret_start(k)
+        ret_start(-k)
+
+    hop(1, 1).start()
+    hop(-1, 1).start()
+    compact_half(0, z)
+    plane_start(0)
+    for k in (1, 2, 3):
+        for sign in (1, -1):
+            arrived(sign, k)
+            hop(sign, k + 1).start()
+        compact_pair(k)
+        plane_start(k)
+        if k == 1:
+            for copy in w_copies:
+                copy.wait()
+            expert_half(0)
+        if k == 3:
+            expert_pair(1)
+    arrived(1, 4)
+    arrived(-1, 4)
+    compact_half(1, at_z(4))
+    plane_start(4)
+    expert_pair(2)
+    expert_pair(3)
+    expert_half(4)
+
+    for sign in (1, -1):
+        for k in (1, 2, 3, 4):
+            hop(sign, k).wait_send()
+    for chunk in range(5):
+        for o in range(1, PLANE):
+            plane_copy(chunk, o).wait_send()
+
+    def ret_sent(i, carry):
+        dz_index = i // PLANE
+        pltpu.make_async_remote_copy(
+            src_ref=ret_out.at[dz_index, i % PLANE],
+            dst_ref=ret_in.at[ep],
+            send_sem=r_send.at[i],
+            recv_sem=r_recv.at[ep],
+            device_id=dev(at_z(dz_index), i % PLANE),
+            device_id_type=MESH,
+        ).wait_send()
+        return carry
+
+    for o in range(1, PLANE):
+        ret_copy(0, (spot + o) % PLANE).wait_send()
+    lax.fori_loop(PLANE, NZ * PLANE, ret_sent, 0)
+
+    def ret_got(o, carry):
+        expert = (ep + o) % (NZ * PLANE)
+        pltpu.make_async_remote_copy(
+            src_ref=ret_in.at[expert],
+            dst_ref=ret_in.at[expert],
+            send_sem=r_send.at[o],
+            recv_sem=r_recv.at[expert],
+            device_id={"ep": expert},
+            device_id_type=MESH,
+        ).wait_recv()
+        return carry
+
+    ret_own().wait()
+    lax.fori_loop(1, NZ * PLANE, ret_got, 0)
+
+    back = ret_in[...].reshape(NZ * PLANE * 16, FFW // 2)
+    column = lax.broadcasted_iota(jnp.int32, (TOK * 8, NZ * PLANE * 16), 1)
+    for half in (0, 1):
+        pick = (column == pos_ref[...] + CAP * half).astype(jnp.float32).astype(jnp.bfloat16)
+        got = jnp.dot(pick, back, preferred_element_type=jnp.float32)
+        out_ref[:, half * (FFW // 2) : (half + 1) * (FFW // 2)] = (
+            share_ref[...] * got
+        ).astype(jnp.bfloat16)
+
+
+def layer_call(rows, gate_weight, up_weight, pos, share):
+    bf = jnp.bfloat16
+    dma = pltpu.SemaphoreType.DMA
+    vmem = pl.BlockSpec(memory_space=pltpu.VMEM)
+    hbm = pl.BlockSpec(memory_space=pl.ANY)
+    return pl.pallas_call(
+        layer_kernel,
+        out_shape=jax.ShapeDtypeStruct((TOK * 8, FFW), bf),
+        in_specs=[vmem, hbm, hbm, vmem, vmem],
+        out_specs=vmem,
+        scratch_shapes=[
+            pltpu.VMEM((NZ, TOK, D + META), bf),
+            pltpu.VMEM((2, PLANE, 16, HALF), bf),
+            pltpu.VMEM((3, PLANE, 16, D), bf),
+            pltpu.VMEM((2, PLANE, 16, HALF), bf),
+            pltpu.VMEM((3, PLANE, 16, D), bf),
+            pltpu.VMEM((D, FFW), bf),
+            pltpu.VMEM((D, FFW), bf),
+            pltpu.VMEM((PLANE, 16, FFW), jnp.float32),
+            pltpu.VMEM((NZ, PLANE, 16, FFW // 2), bf),
+            pltpu.VMEM((NZ * PLANE, 16, FFW // 2), bf),
+            dma((2,)),
+            dma((8,)),
+            dma((8,)),
+            dma((5 * PLANE,)),
+            dma((5 * PLANE,)),
+            dma((NZ * PLANE,)),
+            dma((NZ * PLANE,)),
+        ],
+        compiler_params=pltpu.CompilerParams(
+            collective_id=0, has_side_effects=True, vmem_limit_bytes=48 * 1024 * 1024
+        ),
+        cost_estimate=pl.CostEstimate(
+            flops=2 * 512 * D * 2 * FFW, bytes_accessed=2 * D * FFW * 2, transcendentals=512 * FFW
+        ),
+    )(rows, gate_weight, up_weight, pos, share)
+
+
 def local(
     tokens,
     norm_gain,
@@ -76,36 +387,18 @@
     hidden = (tokens.astype(jnp.float32) + attended.astype(jnp.float32)).astype(jnp.bfloat16)
     normed = rms_rows(hidden, norm_gain)
     experts = lax.axis_size("ep")
-    tok_count = route_ids.shape[0]
-    top_count = route_ids.shape[1]
-    capacity = min(tok_count, 2 * tok_count * top_count // experts)
     expert_ids = jnp.arange(experts, dtype=jnp.int32)
-    slot_ids = jnp.arange(capacity, dtype=jnp.int32)
     route_hot = route_ids[:, :, None] == expert_ids[None, None, :]
     hit_mask = jnp.any(route_hot, axis=1).astype(jnp.int32)
     slot_rank = jnp.cumsum(hit_mask, axis=0) - hit_mask
     row_slot = jnp.sum(jnp.where(route_hot, slot_rank[:, None, :], 0), axis=2)
-    gate_mat = gate_weight[0]
-    up_mat = up_weight[0]
-    placing = (
-        (hit_mask.T[:, None, :] == 1) & (slot_rank.T[:, None, :] == slot_ids[None, :, None])
-    ).astype(jnp.bfloat16)
-    outgoing = jnp.einsum(
-        "est,td->esd", placing, normed, preferred_element_type=jnp.float32
-    ).astype(jnp.bfloat16)
-    received = expert_apply(
-        lax.all_to_all(outgoing, "ep", split_axis=0, concat_axis=0, tiled=True),
-        gate_mat=gate_mat,
-        up_mat=up_mat,
-    )
-    returned = lax.all_to_all(received, "ep", split_axis=0, concat_axis=0, tiled=True)
-    pick_map = (
-        route_hot[:, :, :, None] & (row_slot[:, :, None, None] == slot_ids[None, None, None, :])
-    ).astype(jnp.bfloat16)
-    picked = jnp.einsum("tkes,esf->tkf", pick_map, returned, preferred_element_type=jnp.float32)
+    meta = jnp.where(hit_mask == 1, slot_rank, -1).astype(jnp.bfloat16)
+    meta = jnp.pad(meta, ((0, 0), (0, META - experts)), constant_values=-1)
+    rows = jnp.concatenate([normed, meta], axis=1)
     route_share = route_scores / jnp.sum(route_scores, axis=1, keepdims=True)
-    expert_terms = (route_share[:, :, None] * picked).astype(jnp.bfloat16)
-    return (expert_terms, attended)
+    pos = (route_ids * 16 + row_slot).reshape(-1, 1)
+    expert_terms = layer_call(rows, gate_weight, up_weight, pos, route_share.reshape(-1, 1))
+    return (expert_terms.reshape(route_ids.shape[0], route_ids.shape[1], FFW), attended)
 
 
 def solution(mesh):

time: 156 us -> 90.9 us (0.58)
  blocking collectives: 108 us -> 0 us
  Pallas kernels: 0 us -> 81.8 us
  waiting for transfers between devices: 21.9 us -> 0 us
  matrix products: 12.7 us -> 2.02 us
  starting transfers between devices: 7.02 us -> 0 us
    all_to_all x1 -> x0, blocking collectives: 108 us -> none  [local(): lax.all_to_all(outgoing, 'ep', split_axis=0, concat_axis=0, tiled=True)]
    pallas_call x0 -> x1, Pallas kernels: none -> 81.8 us  [layer_call(): pl.pallas_call(layer_kernel, out_shape=jax.ShapeDtypeStruct((TOK * 8, FFW...]
    all_to_all x1 -> x0, waiting for transfers between devices: 21.9 us -> none  [local(): lax.all_to_all(received, 'ep', split_axis=0, concat_axis=0, tiled=True)]
    dot_general x4 -> x0, matrix products: 10.7 us -> none  [the longest x1 4.45 us: expert_apply(): jnp.einsum('nsd,df->nsf', buffer, up_mat, preferred_element_type=jnp.floa...]
    all_to_all x1 -> x0, starting transfers between devices: 7.02 us -> none  [local(): lax.all_to_all(received, 'ep', split_axis=0, concat_axis=0, tiled=True)]
  transfers between devices with their start and end apart: 1 -> 0, of which waited for: 1 -> 0; matrix products, arithmetic and copies ran while one was open for 1% -> 0% of each run, Pallas kernels for 0% -> 0%
where the time goes in v1:
time: 90.9 us; the launch traced here: 90.6 us
  Pallas kernels  81.8 us (90%)
  local copies, waits for them, and re-layouts  3.58 us (4%)
  other arithmetic  2.4 us (3%)
  matrix products  2.02 us (2%)
    pallas_call x1, Pallas kernels, layer_call(): pl.pallas_call(layer_kernel, out_shape=jax.ShapeDtypeStruct((TOK * 8, FFW...  81.8 us
    unnamed x15, local copies, waits for them, and re-layouts  1.85 us

profile of v1, /device:TPU:1, one launch (start us, length us, event | category | flops | bytes accessed | tf_op | source)
XLA Modules:
  0.0 90.6 jit_solution(9138234357971471864)
XLA Ops:
  0.6 0.0 copy-start
  0.6 0.0 copy-start.1
  0.7 0.0 copy-start.3
  0.7 0.8 iota_compare_fusion.2
  1.5 1.0 %copy.41 = bf16[4,8,32,128]{3,2,1,0:T(8,128)(2,1)S(1)} copy(bf16[4,8,32,128]{3,1,2,0:T(8,128)(2,1)} %bitcast.31) | data formatting | bytes 524288
  2.5 1.3 %fusion.20 = (f32[32,2,16]{2,1,0:T(2,128)S(1)}, f32[32,2,16,16]{2,3,1,0:T(8,128)S(1)}) fusion(bf16[32,2,16,128]{3,2,1,0:T(8,128)(2,1)S(1)} %bitcast.32, pred[32,16]{1,0:T(8,128)(4,1)S(1)} %iota_compare_fusion.2, bf16[32,16,256]{2,1,0:T(8,128)(2,1)} %param.19), kind=kOutput, calls=%fused_computation.40 | convolution fusion | flops 4242432 | bytes 594432 | tf_op jit(solution)/shard_map/tkgd,tckd->tkgc/dot_general | solution.py:36
  3.7 0.7 reshape.77
  4.5 0.2 fusion.21
  4.7 0.2 fusion.6
  5.0 0.1 fusion.19
  5.0 0.7 reshape.73
  5.8 0.0 copy-done
  5.8 0.5 fusion.1
  6.3 0.2 fusion.3
  6.6 0.1 fusion.5
  6.7 0.1 copy.31
  6.8 0.1 fusion.16
  6.9 0.1 reduce_window_sum.11
  7.0 0.7 select_reduce_fusion
  7.7 0.1 reshape.78.pos_ref
  7.9 0.1 copy.33
  8.0 0.1 reshape.79.share_ref
  8.1 81.8 %shard_map.131 = bf16[256,768]{1,0:T(8,128)(2,1)S(1)} custom-call(bf16[32,4224]{1,0:T(8,128)(2,1)S(1)} %fusion.7.rows_ref, bf16[1,4096,768]{2,1,0:T(8,128)(2,1)} %gate_hbm.1, bf16[1,4096,768]{2,1,0:T(8,128)(2,1)} %up_hbm.1, s32[256,1]{1,0:T(8,128)S(1)} %reshape.78.pos_ref, f32[256,1]{1,0:T(8,128)S(1)} %reshape.79.share_ref), custom_call_target="tpu_custom_call" | custom-call | flops 6442450944 | bytes 12582912 | tf_op jit(solution)/shard_map/pallas_call | solution.py:339
  89.8 0.7 copy.56
  (16 shorter events, 0.1 us)
Async XLA Ops:
  0.6 5.1 %copy-start = (bf16[32,16,256]{2,1,0:T(8,128)(2,1)S(1)}, bf16[32,16,256]{2,1,0:T(8,128)(2,1)}, u32[]{:S(2)}) copy-start(bf16[32,16,256]{2,1,0:T(8,128)(2,1)} %param.20) | copy-start | bytes 786436
  0.6 5.7 %copy-start.1 = (bf16[32,4096]{1,0:T(8,128)(2,1)S(1)}, bf16[32,4096]{1,0:T(8,128)(2,1)}, u32[]{:S(2)}) copy-start(bf16[32,4096]{1,0:T(8,128)(2,1)} %param.12) | copy-start | bytes 786436
  0.7 5.9 %copy-start.3 = (f32[4096]{0:T(1024)S(1)}, f32[4096]{0:T(1024)}, u32[]{:S(2)}) copy-start(f32[4096]{0:T(1024)} %param.13) | copy-start | bytes 49156
  0.7 6.1 %copy-start.5 = (s32[32,8]{0,1:T(8,128)S(1)}, s32[32,8]{0,1:T(8,128)}, u32[]{:S(2)}) copy-start(s32[32,8]{0,1:T(8,128)} %param.16) | copy-start | bytes 3076
  0.7 7.2 %copy-start.4 = (f32[32,8]{0,1:T(8,128)S(1)}, f32[32,8]{0,1:T(8,128)}, u32[]{:S(2)}) copy-start(f32[32,8]{0,1:T(8,128)} %param.17) | copy-start | bytes 3076
  6.6 83.3 %copy-start.2 = (bf16[32,4096]{1,0:T(8,128)(2,1)}, bf16[32,4096]{1,0:T(8,128)(2,1)S(1)}, u32[]{:S(2)}) copy-start(bf16[32,4096]{1,0:T(8,128)(2,1)S(1)} %get-tuple-element.13) | copy-start | bytes 786436

commit v2 on v1

v2 whole, which is shorter than its diff:
```python
import jax
import jax.experimental.pallas as pl
import jax.experimental.pallas.tpu as pltpu
import jax.numpy as jnp
from jax import lax
from jax.sharding import PartitionSpec as P

HD = 128
D = 4096
FFW = 768
TOK = 32
CAP = 8
NZ = 8
PLANE = 8
META = 128
HALF = D // 2
MESH = pl.DeviceIdType.MESH


def attend_rows(
    queries_ref, keys_ref, values_ref, new_keys_ref, new_values_ref, lengths_ref, attended_ref
):
    rows, heads = 16, 16
    size = rows * heads
    row = lax.broadcasted_iota(jnp.int32, (size, size), 0) % rows
    lane = lax.broadcasted_iota(jnp.int32, (size, size), 1)
    own_row = lax.broadcasted_iota(jnp.int32, (size, rows), 0) % rows
    own_lane = lax.broadcasted_iota(jnp.int32, (size, rows), 1)
    factor = HD ** (-0.5)
    contract = (((1,), (1,)), ((), ()))
    for first in range(0, TOK, rows):
        part = slice(first, first + rows)
        repeat = (
            lax.broadcasted_iota(jnp.int32, (TOK, size), 0)
            == first + lax.broadcasted_iota(jnp.int32, (TOK, size), 1) // rows
        ).astype(jnp.float32)
        counts = jnp.broadcast_to(lengths_ref[...].astype(jnp.float32), (8, TOK))
        lengths = jnp.dot(counts, repeat, preferred_element_type=jnp.float32)[:1]
        live = (row == lane // rows) & ((lane % rows).astype(jnp.float32) < lengths)
        for kv in range(2):
            cols = slice(kv * HD, (kv + 1) * HD)
            query = jnp.concatenate(
                [
                    queries_ref[part, (kv * heads + g) * HD : (kv * heads + g + 1) * HD]
                    for g in range(heads)
                ],
                axis=0,
            )
            key = keys_ref[part, :, cols].reshape(size, HD)
            value = values_ref[part, :, cols].reshape(size, HD)
            scores = factor * lax.dot_general(
                query, key, contract, preferred_element_type=jnp.float32
            )
            scores = jnp.where(live, scores, -1e30)
            own = factor * lax.dot_general(
                query, new_keys_ref[part, cols], contract, preferred_element_type=jnp.float32
            )
            own = jnp.sum(jnp.where(own_row == own_lane, own, 0.0), axis=1, keepdims=True)
            top = jnp.maximum(jnp.max(scores, axis=1, keepdims=True), own)
            weights = jnp.where(live, jnp.exp(scores - top), 0.0)
            own_weight = jnp.exp(own - top)
            mass = jnp.sum(weights, axis=1, keepdims=True) + own_weight
            probs = (weights / mass).astype(jnp.bfloat16)
            own_prob = (own_weight / mass).astype(jnp.bfloat16).astype(jnp.float32)
            fresh = jnp.concatenate(
                [new_values_ref[part, cols].astype(jnp.float32)] * heads, axis=0
            )
            summed = jnp.dot(probs, value, preferred_element_type=jnp.float32) + own_prob * fresh
            for g in range(heads):
                attended_ref[part, (kv * heads + g) * HD : (kv * heads + g + 1) * HD] = summed[
                    g * rows : (g + 1) * rows
                ].astype(jnp.bfloat16)


def norm_rows(tokens_ref, attended_ref, gain_ref, rows_ref):
    step = 1024
    total = jnp.zeros((TOK, 1), jnp.float32)
    for lo in range(0, D, step):
        cols = slice(lo, lo + step)
        hidden = tokens_ref[:, cols].astype(jnp.float32) + attended_ref[:, cols].astype(
            jnp.float32
        )
        hidden = hidden.astype(jnp.bfloat16)
        rows_ref[:, cols] = hidden
        hidden = hidden.astype(jnp.float32)
        total = total + jnp.sum(hidden * hidden, axis=1, keepdims=True)
    scale = lax.rsqrt(total / D + 1e-06)
    for lo in range(0, D, step):
        cols = slice(lo, lo + step)
        hidden = rows_ref[:, cols].astype(jnp.float32)
        rows_ref[:, cols] = (hidden * scale * gain_ref[:, cols]).astype(jnp.bfloat16)


def slot_ranks(ids_ref):
    expert = lax.broadcasted_iota(jnp.int32, (META, TOK), 0)
    hit = jnp.zeros((META, TOK), jnp.float32)
    for k in range(8):
        hit = hit + (expert == ids_ref[k : k + 1, :]).astype(jnp.float32)
    row = lax.broadcasted_iota(jnp.int32, (TOK, TOK), 0)
    col = lax.broadcasted_iota(jnp.int32, (TOK, TOK), 1)
    hit = hit.astype(jnp.bfloat16)

    def over_rows(mat):
        return lax.dot_general(
            mat.astype(jnp.float32).astype(jnp.bfloat16),
            hit,
            (((1,), (1,)), ((), ())),
            preferred_element_type=jnp.float32,
        )

    by_expert = jnp.dot(
        hit,
        (row < col).astype(jnp.float32).astype(jnp.bfloat16),
        preferred_element_type=jnp.float32,
    )
    meta = jnp.where(over_rows(row == col) > 0.0, over_rows(row > col), -1.0)
    return meta.astype(jnp.bfloat16), by_expert


def pick_columns(ids_ref, scores_ref, rank, pos_col, share_col):
    expert = lax.broadcasted_iota(jnp.int32, (META, TOK), 0)
    slot = jnp.concatenate(
        [
            jnp.sum(jnp.where(expert == ids_ref[k : k + 1, :], rank, 0.0), axis=0, keepdims=True)
            for k in range(8)
        ],
        axis=0,
    )
    score = scores_ref[...]
    share = score / jnp.sum(score, axis=0, keepdims=True)
    spread = (
        lax.broadcasted_iota(jnp.int32, (TOK * 8, TOK), 0) // 8
        == lax.broadcasted_iota(jnp.int32, (TOK * 8, TOK), 1)
    ).astype(jnp.float32)
    mine = lax.broadcasted_iota(jnp.int32, (TOK * 8, 8), 0) % 8 == lax.broadcasted_iota(
        jnp.int32, (TOK * 8, 8), 1
    )

    def column(values):
        every = lax.dot_general(
            spread,
            values,
            (((1,), (1,)), ((), ())),
            precision=lax.Precision.HIGHEST,
            preferred_element_type=jnp.float32,
        )
        return jnp.sum(jnp.where(mine, every, 0.0), axis=1, keepdims=True)

    pos_col[...] = column(ids_ref[...].astype(jnp.float32) * 16.0 + slot).astype(jnp.int32)
    share_col[...] = column(share)


def layer_kernel(
    tokens_hbm, gain_hbm, gate_hbm, up_hbm, ids_hbm, scores_hbm, queries_hbm, keys_hbm,
    values_hbm, new_keys_hbm, new_values_hbm, lengths_hbm, out_ref, attended_ref,
    tokens_ref, gain_ref, ids_ref, scores_ref, queries_ref, keys_ref,
    values_ref, new_keys_ref, new_values_ref, lengths_ref,
    raw, side, half_out, low_out, high_out, half_in, low_in, high_in,
    gate_w, up_w, act, ret_out, ret_in, pos_col, share_col,
    in_sem, w_sem, z_send, z_recv, n_send, n_recv, p_send, p_recv, h_send, h_recv, r_send, r_recv,
):
    ep = lax.axis_index("ep")
    z = ep // PLANE
    spot = ep % PLANE
    x = spot // 2
    core = spot % 2
    turn = 1 - 2 * core

    def at_x(steps):
        return (x + steps * turn + 4) % 4

    def spot_of(steps, other):
        return at_x(steps) * 2 + (core + other) % 2

    def at_z(dz):
        return (z + dz + NZ) % NZ

    def dev(zz, ss):
        return {"ep": zz * PLANE + ss}

    in_copies = [
        pltpu.make_async_copy(source, target, in_sem.at[i])
        for i, (source, target) in enumerate(
            (
                (queries_hbm, queries_ref),
                (keys_hbm, keys_ref),
                (values_hbm, values_ref),
                (new_keys_hbm, new_keys_ref),
                (new_values_hbm, new_values_ref),
                (lengths_hbm, lengths_ref),
                (tokens_hbm, tokens_ref),
                (gain_hbm, gain_ref),
                (ids_hbm, ids_ref),
                (scores_hbm, scores_ref),
            )
        )
    ]
    w_copies = [
        pltpu.make_async_copy(gate_hbm.at[0], gate_w, w_sem.at[0]),
        pltpu.make_async_copy(up_hbm.at[0], up_w, w_sem.at[1]),
    ]
    for copy in in_copies + w_copies:
        copy.start()
    barrier = pltpu.get_barrier_semaphore()

    def greet(o, carry):
        pl.semaphore_signal(
            barrier, inc=1, device_id={"ep": (ep + o) % (NZ * PLANE)}, device_id_type=MESH
        )
        return carry

    lax.fori_loop(1, NZ * PLANE, greet, 0)
    for copy in in_copies:
        copy.wait()
    attend_rows(
        queries_ref, keys_ref, values_ref, new_keys_ref, new_values_ref, lengths_ref, attended_ref
    )
    norm_rows(tokens_ref, attended_ref, gain_ref, raw.at[z])
    meta, rank = slot_ranks(ids_ref)
    raw[z, :, D:] = meta
    pl.semaphore_wait(barrier, NZ * PLANE - 1)

    def hop(sign, k):
        block = raw.at[at_z(-sign * (k - 1))]
        if k == 4:
            block = block.at[pl.ds(0 if sign > 0 else 16, 16)]
        idx = (k - 1) + (0 if sign > 0 else 4)
        return pltpu.make_async_remote_copy(
            src_ref=block,
            dst_ref=block,
            send_sem=z_send.at[idx],
            recv_sem=z_recv.at[idx],
            device_id=dev(at_z(sign), spot),
            device_id_type=MESH,
        )

    def arrived(sign, k):
        block = raw.at[at_z(-sign * k)]
        if k == 4:
            block = block.at[pl.ds(0 if sign > 0 else 16, 16)]
        idx = (k - 1) + (0 if sign > 0 else 4)
        pltpu.make_async_remote_copy(
            src_ref=block,
            dst_ref=block,
            send_sem=z_send.at[idx],
            recv_sem=z_recv.at[idx],
            device_id=dev(at_z(sign), spot),
            device_id_type=MESH,
        ).wait_recv()

    def side_copy(idx, block_out, block_in, device):
        return pltpu.make_async_remote_copy(
            src_ref=block_out,
            dst_ref=block_in,
            send_sem=n_send.at[idx],
            recv_sem=n_recv.at[idx],
            device_id=device,
            device_id_type=MESH,
        )

    def side_first():
        return side_copy(
            0, raw.at[z, :, pl.ds(HALF, HALF + META)], side.at[z], dev(z, spot_of(1, 0))
        )

    def side_hop(sign, k):
        block = side.at[at_z(-sign * (k - 1))]
        return side_copy(k if sign > 0 else k + 3, block, block, dev(at_z(sign), spot))

    def side_arrived(sign, k):
        block = side.at[at_z(-sign * k)]
        side_copy(k if sign > 0 else k + 3, block, block, dev(at_z(sign), spot)).wait_recv()

    def expert_hot(near, far):
        slot_row = lax.broadcasted_iota(jnp.int32, (4 * CAP, META), 0) // CAP
        lane = lax.broadcasted_iota(jnp.int32, (4 * CAP, META), 1)
        spots = jnp.where(slot_row < 2, near * 2 + slot_row, far * 2 + slot_row - 2)
        return (lane == z * PLANE + spots).astype(jnp.bfloat16)

    slot_row = lax.broadcasted_iota(jnp.int32, (PLANE * CAP, META), 0)
    lane = lax.broadcasted_iota(jnp.int32, (PLANE * CAP, META), 1)
    plane_hot = (lane == z * PLANE + slot_row // CAP).astype(jnp.bfloat16)
    own_hot = expert_hot(x, at_x(-1))
    side_hot = expert_hot(x, at_x(1))

    def placing(hot, meta):
        ranks = lax.dot_general(
            hot, meta, (((1,), (1,)), ((), ())), preferred_element_type=jnp.float32
        )
        wanted = lax.broadcasted_iota(jnp.int32, ranks.shape, 0) % CAP
        return (ranks == wanted.astype(jnp.float32)).astype(jnp.float32).astype(jnp.bfloat16)

    def slots(place, block):
        got = jnp.dot(place, block, preferred_element_type=jnp.float32)
        return got.reshape(place.shape[0] // CAP, CAP, block.shape[1])

    def compact_half(i, zz):
        place = placing(plane_hot, raw[zz, :, D:])
        for lo in range(0, HALF, 1024):
            both = jnp.concatenate(
                [
                    slots(place, raw[zz, :, lo : lo + 1024]),
                    slots(place, raw[zz, :, HALF + lo : HALF + lo + 1024]),
                ],
                axis=1,
            )
            half_out[i, :, :, lo : lo + 1024] = both.astype(jnp.bfloat16)

    def compact_pair(k, hot, source, meta_at, first, out, place_at):
        upper, lower = at_z(k), at_z(-k)
        place_u = placing(hot, source[upper, :, meta_at : meta_at + META])
        place_l = placing(hot, source[lower, :, meta_at : meta_at + META])
        for lo in range(0, HALF, 1024):
            both = jnp.concatenate(
                [
                    slots(place_u, source[upper, :, first + lo : first + lo + 1024]),
                    slots(place_l, source[lower, :, first + lo : first + lo + 1024]),
                ],
                axis=1,
            )
            rows = hot.shape[0] // CAP
            out[k - 1, place_at : place_at + rows, :, lo : lo + 1024] = both.astype(jnp.bfloat16)

    def plane_refs(chunk):
        if chunk in (0, 4):
            return half_out.at[chunk // 4], half_in.at[chunk // 4]
        return low_out.at[chunk - 1], low_in.at[chunk - 1]

    def plane_copy(chunk, o):
        outgoing, incoming = plane_refs(chunk)
        target = (spot + o) % PLANE
        return pltpu.make_async_remote_copy(
            src_ref=outgoing.at[target],
            dst_ref=incoming.at[spot],
            send_sem=p_send.at[chunk * PLANE + target],
            recv_sem=p_recv.at[chunk * PLANE + spot],
            device_id=dev(z, target),
            device_id_type=MESH,
        )

    def plane_own(chunk):
        outgoing, incoming = plane_refs(chunk)
        return pltpu.make_async_copy(
            outgoing.at[spot], incoming.at[spot], p_recv.at[chunk * PLANE + spot]
        )

    def plane_start(chunk):
        for o in range(1, PLANE):
            plane_copy(chunk, o).start()
        plane_own(chunk).start()

    def plane_wait(chunk):
        outgoing, incoming = plane_refs(chunk)
        for o in range(1, PLANE):
            source = (spot + o) % PLANE
            pltpu.make_async_remote_copy(
                src_ref=outgoing.at[source],
                dst_ref=incoming.at[source],
                send_sem=p_send.at[chunk * PLANE + source],
                recv_sem=p_recv.at[chunk * PLANE + source],
                device_id=dev(z, source),
                device_id_type=MESH,
            ).wait_recv()
        plane_own(chunk).wait()

    def high_copy(k, place, steps, other, origin):
        return pltpu.make_async_remote_copy(
            src_ref=high_out.at[k - 1, place],
            dst_ref=high_in.at[k - 1, origin],
            send_sem=h_send.at[(k - 1) * PLANE + place],
            recv_sem=h_recv.at[(k - 1) * PLANE + origin],
            device_id=dev(z, spot_of(steps, other)),
            device_id_type=MESH,
        )

    def high_local(k, place, origin):
        return pltpu.make_async_copy(
            high_out.at[k - 1, place],
            high_in.at[k - 1, origin],
            h_recv.at[(k - 1) * PLANE + origin],
        )

    def high_list(k, base, far, origin):
        return [
            high_copy(k, base + (core + 1) % 2, 0, 1, origin),
            high_copy(k, base + 2 + core, far, 0, origin),
            high_copy(k, base + 2 + (core + 1) % 2, far, 1, origin),
        ]

    def high_own(k):
        return high_list(k, 0, -1, spot)

    def high_side(k):
        return high_list(k, 4, 1, spot_of(-1, 0))

    def high_start(k, base, copies, origin):
        for copy in copies:
            copy.start()
        high_local(k, base + core, origin).start()

    def high_wait(k):
        for steps, other in ((1, 0), (2, 0), (0, 1), (1, 1), (2, 1), (3, 1)):
            high_copy(k, 0, 0, 1, spot_of(steps, other)).wait_recv()
        high_local(k, core, spot).wait()
        high_local(k, 4 + core, spot_of(-1, 0)).wait()

    def gated(gate_val, up_val):
        return gate_val / (1.0 + jnp.exp(-gate_val)) * up_val

    def give_back(values, dz_index):
        both = jnp.concatenate([values[:, :, : FFW // 2], values[:, :, FFW // 2 :]], axis=1)
        ret_out[dz_index] = both.astype(jnp.bfloat16)

    def ret_copy(dz, r):
        idx = (dz + NZ) % NZ
        return pltpu.make_async_remote_copy(
            src_ref=ret_out.at[idx, r],
            dst_ref=ret_in.at[ep],
            send_sem=r_send.at[idx * PLANE + r],
            recv_sem=r_recv.at[ep],
            device_id=dev(at_z(dz), r),
            device_id_type=MESH,
        )

    def ret_own():
        return pltpu.make_async_copy(ret_out.at[0, spot], ret_in.at[ep], r_recv.at[ep])

    def ret_start(dz):
        for o in range(PLANE):
            if dz == 0 and o == 0:
                ret_own().start()
            else:
                ret_copy(dz, (spot + o) % PLANE).start()

    def expert_half(chunk):
        plane_wait(chunk)
        for lo in range(0, FFW, 256):
            rows = half_in[chunk // 4].reshape(PLANE * 16, HALF)

            def halves(mat):
                first = jnp.dot(
                    rows, mat[:HALF, lo : lo + 256], preferred_element_type=jnp.float32
                ).reshape(PLANE, 16, 256)
                second = jnp.dot(
                    rows, mat[HALF:, lo : lo + 256], preferred_element_type=jnp.float32
                ).reshape(PLANE, 16, 256)
                return first[:, :CAP] + second[:, CAP:]

            act[:, :CAP, lo : lo + 256] = gated(halves(gate_w), halves(up_w))
        give_back(act[:, :CAP], chunk)
        ret_start(chunk)

    def expert_pair(k):
        plane_wait(k)
        high_wait(k)
        for lo in range(0, FFW, 256):
            low = low_in[k - 1].reshape(PLANE * 16, HALF)
            high = high_in[k - 1].reshape(PLANE * 16, HALF)

            def both(mat):
                return jnp.dot(
                    low, mat[:HALF, lo : lo + 256], preferred_element_type=jnp.float32
                ) + jnp.dot(high, mat[HALF:, lo : lo + 256], preferred_element_type=jnp.float32)

            act[:, :, lo : lo + 256] = gated(both(gate_w), both(up_w)).reshape(PLANE, 16, 256)
        give_back(act[:, :CAP], k)
        give_back(act[:, CAP:], NZ - k)
        ret_start(k)
        ret_start(-k)

    hop(1, 1).start()
    hop(-1, 1).start()
    side_first().start()
    compact_half(0, z)
    plane_start(0)
    pick_columns(ids_ref, scores_ref, rank, pos_col, share_col)
    side_copy(0, side.at[z], side.at[z], dev(z, spot_of(1, 0))).wait_recv()
    side_hop(1, 1).start()
    side_hop(-1, 1).start()
    for k in (1, 2, 3):
        for sign in (1, -1):
            arrived(sign, k)
            hop(sign, k + 1).start()
        compact_pair(k, plane_hot, raw, D, 0, low_out, 0)
        plane_start(k)
        compact_pair(k, own_hot, raw, D, HALF, high_out, 0)
        high_start(k, 0, high_own(k), spot)
        for sign in (1, -1):
            side_arrived(sign, k)
            if k < 3:
                side_hop(sign, k + 1).start()
        compact_pair(k, side_hot, side, HALF, 0, high_out, 4)
        high_start(k, 4, high_side(k), spot_of(-1, 0))
        if k == 1:
            for copy in w_copies:
                copy.wait()
            expert_half(0)
        else:
            expert_pair(k - 1)
    arrived(1, 4)
    arrived(-1, 4)
    compact_half(1, at_z(4))
    plane_start(4)
    expert_pair(3)
    expert_half(4)

    side_first().wait_send()
    for sign in (1, -1):
        for k in (1, 2, 3, 4):
            hop(sign, k).wait_send()
        for k in (1, 2, 3):
            side_hop(sign, k).wait_send()
    for k in (1, 2, 3):
        for copy in high_own(k) + high_side(k):
            copy.wait_send()
    for chunk in range(5):
        for o in range(1, PLANE):
            plane_copy(chunk, o).wait_send()

    def ret_sent(i, carry):
        dz_index = i // PLANE
        pltpu.make_async_remote_copy(
            src_ref=ret_out.at[dz_index, i % PLANE],
            dst_ref=ret_in.at[ep],
            send_sem=r_send.at[i],
            recv_sem=r_recv.at[ep],
            device_id=dev(at_z(dz_index), i % PLANE),
            device_id_type=MESH,
        ).wait_send()
        return carry

    for o in range(1, PLANE):
        ret_copy(0, (spot + o) % PLANE).wait_send()
    lax.fori_loop(PLANE, NZ * PLANE, ret_sent, 0)

    def ret_got(o, carry):
        expert = (ep + o) % (NZ * PLANE)
        pltpu.make_async_remote_copy(
            src_ref=ret_in.at[expert],
            dst_ref=ret_in.at[expert],
            send_sem=r_send.at[o],
            recv_sem=r_recv.at[expert],
            device_id={"ep": expert},
            device_id_type=MESH,
        ).wait_recv()
        return carry

    ret_own().wait()
    lax.fori_loop(1, NZ * PLANE, ret_got, 0)

    back = ret_in[...].reshape(NZ * PLANE * 16, FFW // 2)
    column = lax.broadcasted_iota(jnp.int32, (TOK * 8, NZ * PLANE * 16), 1)
    for half in (0, 1):
        pick = (column == pos_col[...] + CAP * half).astype(jnp.float32).astype(jnp.bfloat16)
        got = jnp.dot(pick, back, preferred_element_type=jnp.float32)
        out_ref[:, half * (FFW // 2) : (half + 1) * (FFW // 2)] = (
            share_col[...] * got
        ).astype(jnp.bfloat16)


def layer_call(*args):
    bf = jnp.bfloat16
    dma = pltpu.SemaphoreType.DMA
    vmem = pl.BlockSpec(memory_space=pltpu.VMEM)
    hbm = pl.BlockSpec(memory_space=pl.ANY)
    return pl.pallas_call(
        layer_kernel,
        out_shape=(
            jax.ShapeDtypeStruct((TOK * 8, FFW), bf),
            jax.ShapeDtypeStruct((TOK, D), bf),
        ),
        in_specs=[hbm] * 12,
        out_specs=(vmem, vmem),
        scratch_shapes=[
            pltpu.VMEM((TOK, D), bf),
            pltpu.VMEM((1, D), jnp.float32),
            pltpu.VMEM((8, TOK), jnp.int32),
            pltpu.VMEM((8, TOK), jnp.float32),
            pltpu.VMEM((TOK, D), bf),
            pltpu.VMEM((TOK, 16, 2 * HD), bf),
            pltpu.VMEM((TOK, 16, 2 * HD), bf),
            pltpu.VMEM((TOK, 2 * HD), bf),
            pltpu.VMEM((TOK, 2 * HD), bf),
            pltpu.VMEM((1, TOK), jnp.int32),
            pltpu.VMEM((NZ, TOK, D + META), bf),
            pltpu.VMEM((NZ, TOK, HALF + META), bf),
            pltpu.VMEM((2, PLANE, 16, HALF), bf),
            pltpu.VMEM((3, PLANE, 16, HALF), bf),
            pltpu.VMEM((3, PLANE, 16, HALF), bf),
            pltpu.VMEM((2, PLANE, 16, HALF), bf),
            pltpu.VMEM((3, PLANE, 16, HALF), bf),
            pltpu.VMEM((3, PLANE, 16, HALF), bf),
            pltpu.VMEM((D, FFW), bf),
            pltpu.VMEM((D, FFW), bf),
            pltpu.VMEM((PLANE, 16, FFW), jnp.float32),
            pltpu.VMEM((NZ, PLANE, 16, FFW // 2), bf),
            pltpu.VMEM((NZ * PLANE, 16, FFW // 2), bf),
            pltpu.VMEM((TOK * 8, 1), jnp.int32),
            pltpu.VMEM((TOK * 8, 1), jnp.float32),
            dma((10,)),
            dma((2,)),
            dma((8,)),
            dma((8,)),
            dma((7,)),
            dma((7,)),
            dma((5 * PLANE,)),
            dma((5 * PLANE,)),
            dma((3 * PLANE,)),
            dma((3 * PLANE,)),
            dma((NZ * PLANE,)),
            dma((NZ * PLANE,)),
        ],
        compiler_params=pltpu.CompilerParams(
            collective_id=0, has_side_effects=True, vmem_limit_bytes=60 * 1024 * 1024
        ),
        cost_estimate=pl.CostEstimate(
            flops=2 * 512 * D * 2 * FFW, bytes_accessed=2 * D * FFW * 2, transcendentals=512 * FFW
        ),
    )(*args)


def hand_over_kernel(terms_in, attended_in, terms_out, attended_out, terms_buf, attended_buf, sem):
    arriving, leaving = [], []
    for source, middle, target in (
        (terms_in, terms_buf, terms_out),
        (attended_in, attended_buf, attended_out),
    ):
        step = source.shape[0] // 2
        for part in range(2):
            rows = pl.ds(part * step, step)
            i = 2 * len(arriving)
            arriving.append(pltpu.make_async_copy(source.at[rows], middle.at[rows], sem.at[i]))
            leaving.append(pltpu.make_async_copy(middle.at[rows], target.at[rows], sem.at[i + 1]))
    for copy in arriving:
        copy.start()
    for first, second in zip(arriving, leaving):
        first.wait()
        second.start()
    for copy in leaving:
        copy.wait()


def hand_over(terms, attended):
    hbm = pl.BlockSpec(memory_space=pl.ANY)
    return pl.pallas_call(
        hand_over_kernel,
        out_shape=(
            jax.ShapeDtypeStruct(terms.shape, terms.dtype),
            jax.ShapeDtypeStruct(attended.shape, attended.dtype),
        ),
        in_specs=[hbm, hbm],
        out_specs=(hbm, hbm),
        scratch_shapes=[
            pltpu.VMEM(terms.shape, terms.dtype),
            pltpu.VMEM(attended.shape, attended.dtype),
            pltpu.SemaphoreType.DMA((8,)),
        ],
        compiler_params=pltpu.CompilerParams(vmem_limit_bytes=60 * 1024 * 1024),
    )(terms, attended)


def local(
    tokens,
    norm_gain,
    gate_weight,
    up_weight,
    route_ids,
    route_scores,
    queries,
    key_cache,
    value_cache,
    new_keys,
    new_values,
    cache_lengths,
):
    expert_terms, attended = layer_call(
        tokens,
        norm_gain.reshape(1, -1),
        gate_weight,
        up_weight,
        route_ids.T,
        route_scores.T,
        queries,
        key_cache,
        value_cache,
        new_keys,
        new_values,
        cache_lengths.reshape(1, -1),
    )
    expert_terms, attended = hand_over(expert_terms, attended)
    return (expert_terms.reshape(route_ids.shape[0], route_ids.shape[1], FFW), attended)


def solution(mesh):
    return jax.shard_map(
        local,
        mesh=mesh,
        in_specs=(
            P(("rep", "ep"), None),
            P(),
            P(("rep", "ep"), None, None),
            P(("rep", "ep"), None, None),
            P(("rep", "ep"), None),
            P(("rep", "ep"), None),
            P(("rep", "ep"), None),
            P(("rep", "ep"), None, None),
            P(("rep", "ep"), None, None),
            P(("rep", "ep"), None),
            P(("rep", "ep"), None),
            P(("rep", "ep")),
        ),
        out_specs=(P(("rep", "ep"), None, None), P(("rep", "ep"), None)),
        check_vma=False,
    )
```

time: 90.9 us -> 76.5 us (0.84)
  Pallas kernels: 81.8 us -> 75.4 us
  local copies, waits for them, and re-layouts: 3.58 us -> 0 us
  other arithmetic: 2.4 us -> 0 us
  matrix products: 2.02 us -> 0 us
    pallas_call x1 -> x2, Pallas kernels: 81.8 us -> 75.4 us  [the longest x1 73.5 us: layer_call(): pl.pallas_call(layer_kernel, out_shape=(jax.ShapeDtypeStruct((TOK * 8, FF...]
    dot_general x3 -> x0, matrix products: 2.02 us -> none  [the longest x1 1.25 us: attend_rows(): jnp.einsum('tkgd,tckd->tkgc', query_heads, key_heads, preferred_element_t...]
    unnamed x15 -> x0, local copies, waits for them, and re-layouts: 1.85 us -> none
    reduce_sum x4 -> x0, other arithmetic: 1.18 us -> none  [the longest x1 0.68 us: local(): row_slot = jnp.sum(jnp.where(route_hot, slot_rank[:, None, :], 0), axis=2)]
    reshape x3 -> x0, local copies, waits for them, and re-layouts: 0.92 us -> none  [the longest x1 0.73 us: attend_rows(): new_keys.reshape(row_count, kv_heads, HD)]
where the time goes in v2:
time: 76.5 us; the launch traced here: 76.2 us
  Pallas kernels  75.4 us (99%)
  between operations  0.8 us (1%)
    pallas_call x1, Pallas kernels, layer_call(): pl.pallas_call(layer_kernel, out_shape=(jax.ShapeDtypeStruct((TOK * 8, FF...  73.5 us
    pallas_call x1, Pallas kernels, hand_over(): pl.pallas_call(hand_over_kernel, out_shape=(jax.ShapeDtypeStruct(terms.sh...  1.89 us

profile of v2, /device:TPU:1, one launch (start us, length us, event | category | flops | bytes accessed | tf_op | source)
XLA Modules:
  0.0 76.2 jit_solution(3819550873829675639)
XLA Ops:
  0.6 73.5 %shard_map.131 = (bf16[256,768]{1,0:T(8,128)(2,1)}, bf16[32,4096]{1,0:T(8,128)(2,1)}) custom-call(bf16[32,4096]{1,0:T(8,128)(2,1)} %tokens_hbm.1, f32[1,4096]{1,0:T(1,128)} %bitcast.6, bf16[1,4096,768]{2,1,0:T(8,128)(2,1)} %gate_hbm.1, bf16[1,4096,768]{2,1,0:T(8,128)(2,1)} %up_hbm.1, s32[8,32]{1,0:T(8,128)} %bitcast.7, f32[8,32]{1,0:T(8,128)} %bitcast.8, ...), custom_call_target="tpu_custom_call" | custom-call | flops 6442450944 | bytes 12582912 | tf_op jit(solution)/shard_map/pallas_call | solution.py:566
  74.1 1.9 %shard_map.132 = (bf16[256,768]{1,0:T(8,128)(2,1)}, bf16[32,4096]{1,0:T(8,128)(2,1)}) custom-call(bf16[256,768]{1,0:T(8,128)(2,1)} %get-tuple-element.6.terms_in, bf16[32,4096]{1,0:T(8,128)(2,1)} %get-tuple-element.7.attended_in), custom_call_target="tpu_custom_call" | custom-call | tf_op jit(solution)/shard_map/pallas_call | solution.py:645

commit v3 on v2

--- a/solution.py
+++ b/solution.py
@@ -203,13 +203,12 @@
         copy.start()
     barrier = pltpu.get_barrier_semaphore()
 
-    def greet(o, carry):
+    for sign in (1, -1):
+        pl.semaphore_signal(barrier, inc=1, device_id=dev(at_z(sign), spot), device_id_type=MESH)
+    for o in range(1, PLANE):
         pl.semaphore_signal(
-            barrier, inc=1, device_id={"ep": (ep + o) % (NZ * PLANE)}, device_id_type=MESH
-        )
-        return carry
-
-    lax.fori_loop(1, NZ * PLANE, greet, 0)
+            barrier, inc=1, device_id=dev(z, (spot + o) % PLANE), device_id_type=MESH
+        )
     for copy in in_copies:
         copy.wait()
     attend_rows(
@@ -218,7 +217,7 @@
     norm_rows(tokens_ref, attended_ref, gain_ref, raw.at[z])
     meta, rank = slot_ranks(ids_ref)
     raw[z, :, D:] = meta
-    pl.semaphore_wait(barrier, NZ * PLANE - 1)
+    pl.semaphore_wait(barrier, PLANE + 1)
 
     def hop(sign, k):
         block = raw.at[at_z(-sign * (k - 1))]
@@ -477,26 +476,46 @@
     side_copy(0, side.at[z], side.at[z], dev(z, spot_of(1, 0))).wait_recv()
     side_hop(1, 1).start()
     side_hop(-1, 1).start()
-    for k in (1, 2, 3):
-        for sign in (1, -1):
-            arrived(sign, k)
-            hop(sign, k + 1).start()
-        compact_pair(k, plane_hot, raw, D, 0, low_out, 0)
-        plane_start(k)
-        compact_pair(k, own_hot, raw, D, HALF, high_out, 0)
-        high_start(k, 0, high_own(k), spot)
-        for sign in (1, -1):
-            side_arrived(sign, k)
-            if k < 3:
-                side_hop(sign, k + 1).start()
-        compact_pair(k, side_hot, side, HALF, 0, high_out, 4)
-        high_start(k, 4, high_side(k), spot_of(-1, 0))
-        if k == 1:
-            for copy in w_copies:
-                copy.wait()
-            expert_half(0)
-        else:
-            expert_pair(k - 1)
+    for sign in (1, -1):
+        arrived(sign, 1)
+        hop(sign, 1 + 1).start()
+    compact_pair(1, plane_hot, raw, D, 0, low_out, 0)
+    plane_start(1)
+    compact_pair(1, own_hot, raw, D, HALF, high_out, 0)
+    high_start(1, 0, high_own(1), spot)
+    for sign in (1, -1):
+        side_arrived(sign, 1)
+        side_hop(sign, 1 + 1).start()
+    compact_pair(1, side_hot, side, HALF, 0, high_out, 4)
+    high_start(1, 4, high_side(1), spot_of(-1, 0))
+    for copy in w_copies:
+        copy.wait()
+    expert_half(0)
+    for sign in (1, -1):
+        arrived(sign, 2)
+        hop(sign, 2 + 1).start()
+    compact_pair(2, plane_hot, raw, D, 0, low_out, 0)
+    plane_start(2)
+    compact_pair(2, own_hot, raw, D, HALF, high_out, 0)
+    high_start(2, 0, high_own(2), spot)
+    for sign in (1, -1):
+        side_arrived(sign, 2)
+        side_hop(sign, 2 + 1).start()
+    compact_pair(2, side_hot, side, HALF, 0, high_out, 4)
+    high_start(2, 4, high_side(2), spot_of(-1, 0))
+    expert_pair(1)
+    for sign in (1, -1):
+        arrived(sign, 3)
+        hop(sign, 3 + 1).start()
+    compact_pair(3, plane_hot, raw, D, 0, low_out, 0)
+    plane_start(3)
+    compact_pair(3, own_hot, raw, D, HALF, high_out, 0)
+    high_start(3, 0, high_own(3), spot)
+    expert_pair(2)
+    for sign in (1, -1):
+        side_arrived(sign, 3)
+    compact_pair(3, side_hot, side, HALF, 0, high_out, 4)
+    high_start(3, 4, high_side(3), spot_of(-1, 0))
     arrived(1, 4)
     arrived(-1, 4)
     compact_half(1, at_z(4))

time: 76.5 us -> 74.9 us (0.979)
  Pallas kernels: 75.4 us -> 74.2 us
    pallas_call x1, Pallas kernels: 73.5 us -> 72.3 us  [layer_call(): pl.pallas_call(layer_kernel, out_shape=(jax.ShapeDtypeStruct((TOK * 8, FF...]
where the time goes in v3:
time: 74.9 us; the launch traced here: 74.8 us
  Pallas kernels  74.2 us (99%)
    pallas_call x1, Pallas kernels, layer_call(): pl.pallas_call(layer_kernel, out_shape=(jax.ShapeDtypeStruct((TOK * 8, FF...  72.3 us
    pallas_call x1, Pallas kernels, hand_over(): pl.pallas_call(hand_over_kernel, out_shape=(jax.ShapeDtypeStruct(terms.sh...  1.89 us

profile of v3, /device:TPU:1, one launch (start us, length us, event | category | flops | bytes accessed | tf_op | source)
XLA Modules:
  0.0 74.8 jit_solution(11603047031222047915)
XLA Ops:
  0.6 72.3 %shard_map.131 = (bf16[256,768]{1,0:T(8,128)(2,1)}, bf16[32,4096]{1,0:T(8,128)(2,1)}) custom-call(bf16[32,4096]{1,0:T(8,128)(2,1)} %tokens_hbm.1, f32[1,4096]{1,0:T(1,128)} %bitcast.6, bf16[1,4096,768]{2,1,0:T(8,128)(2,1)} %gate_hbm.1, bf16[1,4096,768]{2,1,0:T(8,128)(2,1)} %up_hbm.1, s32[8,32]{1,0:T(8,128)} %bitcast.7, f32[8,32]{1,0:T(8,128)} %bitcast.8, ...), custom_call_target="tpu_custom_call" | custom-call | flops 6442450944 | bytes 12582912 | tf_op jit(solution)/shard_map/pallas_call | solution.py:585
  72.9 1.9 %shard_map.132 = (bf16[256,768]{1,0:T(8,128)(2,1)}, bf16[32,4096]{1,0:T(8,128)(2,1)}) custom-call(bf16[256,768]{1,0:T(8,128)(2,1)} %get-tuple-element.6.terms_in, bf16[32,4096]{1,0:T(8,128)(2,1)} %get-tuple-element.7.attended_in), custom_call_target="tpu_custom_call" | custom-call | tf_op jit(solution)/shard_map/pallas_call | solution.py:664

commit v4 on v3

--- a/solution.py
+++ b/solution.py
@@ -156,7 +156,7 @@
     tokens_ref, gain_ref, ids_ref, scores_ref, queries_ref, keys_ref,
     values_ref, new_keys_ref, new_values_ref, lengths_ref,
     raw, side, half_out, low_out, high_out, half_in, low_in, high_in,
-    gate_w, up_w, act, ret_out, ret_in, pos_col, share_col,
+    gate_w, up_w, act, ret_out, ret_in, pos_col, share_col, picked,
     in_sem, w_sem, z_send, z_recv, n_send, n_recv, p_send, p_recv, h_send, h_recv, r_send, r_recv,
 ):
     ep = lax.axis_index("ep")
@@ -523,6 +523,41 @@
     expert_pair(3)
     expert_half(4)
 
+    def ret_got(o, plane):
+        expert = plane * PLANE + (spot + o) % PLANE
+        pltpu.make_async_remote_copy(
+            src_ref=ret_in.at[expert],
+            dst_ref=ret_in.at[expert],
+            send_sem=r_send.at[o],
+            recv_sem=r_recv.at[expert],
+            device_id=dev((plane + 1) % NZ, spot),
+            device_id_type=MESH,
+        ).wait_recv()
+        return plane
+
+    column = lax.broadcasted_iota(jnp.int32, (TOK * 8, PLANE * 16), 1)
+
+    def gather(planes, last):
+        for dz in planes:
+            if dz == 0:
+                ret_own().wait()
+            lax.fori_loop(1 if dz == 0 else 0, PLANE, ret_got, at_z(dz))
+        for half in (0, 1):
+            cols = slice(half * (FFW // 2), (half + 1) * (FFW // 2))
+            got = jnp.zeros((TOK * 8, FFW // 2), jnp.float32)
+            for dz in planes:
+                base = at_z(dz) * PLANE * 16 - CAP * half
+                pick = (column + base == pos_col[...]).astype(jnp.float32).astype(jnp.bfloat16)
+                back = ret_in[pl.ds(at_z(dz) * PLANE, PLANE)].reshape(PLANE * 16, FFW // 2)
+                got = got + jnp.dot(pick, back, preferred_element_type=jnp.float32)
+            if last:
+                got = share_col[...] * (picked[:, cols] + got)
+                out_ref[:, cols] = got.astype(jnp.bfloat16)
+            else:
+                picked[:, cols] = got
+
+    far_planes = (3, -3, 4)
+    gather((0, 1, -1, 2, -2), False)
     side_first().wait_send()
     for sign in (1, -1):
         for k in (1, 2, 3, 4):
@@ -552,29 +587,7 @@
         ret_copy(0, (spot + o) % PLANE).wait_send()
     lax.fori_loop(PLANE, NZ * PLANE, ret_sent, 0)
 
-    def ret_got(o, carry):
-        expert = (ep + o) % (NZ * PLANE)
-        pltpu.make_async_remote_copy(
-            src_ref=ret_in.at[expert],
-            dst_ref=ret_in.at[expert],
-            send_sem=r_send.at[o],
-            recv_sem=r_recv.at[expert],
-            device_id={"ep": expert},
-            device_id_type=MESH,
-        ).wait_recv()
-        return carry
-
-    ret_own().wait()
-    lax.fori_loop(1, NZ * PLANE, ret_got, 0)
-
-    back = ret_in[...].reshape(NZ * PLANE * 16, FFW // 2)
-    column = lax.broadcasted_iota(jnp.int32, (TOK * 8, NZ * PLANE * 16), 1)
-    for half in (0, 1):
-        pick = (column == pos_col[...] + CAP * half).astype(jnp.float32).astype(jnp.bfloat16)
-        got = jnp.dot(pick, back, preferred_element_type=jnp.float32)
-        out_ref[:, half * (FFW // 2) : (half + 1) * (FFW // 2)] = (
-            share_col[...] * got
-        ).astype(jnp.bfloat16)
+    gather(far_planes, True)
 
 
 def layer_call(*args):
@@ -616,6 +629,7 @@
             pltpu.VMEM((NZ * PLANE, 16, FFW // 2), bf),
             pltpu.VMEM((TOK * 8, 1), jnp.int32),
             pltpu.VMEM((TOK * 8, 1), jnp.float32),
+            pltpu.VMEM((TOK * 8, FFW), jnp.float32),
             dma((10,)),
             dma((2,)),
             dma((8,)),

time: 74.9 us -> 74.7 us (level)
  no operation moved by 1% of the time
where the time goes in v4:
time: 74.7 us; the launch traced here: 74.6 us
  Pallas kernels  73.9 us (99%)
    pallas_call x1, Pallas kernels, layer_call(): pl.pallas_call(layer_kernel, out_shape=(jax.ShapeDtypeStruct((TOK * 8, FF...  72 us
    pallas_call x1, Pallas kernels, hand_over(): pl.pallas_call(hand_over_kernel, out_shape=(jax.ShapeDtypeStruct(terms.sh...  1.89 us

profile of v4, /device:TPU:1, one launch (start us, length us, event | category | flops | bytes accessed | tf_op | source)
XLA Modules:
  0.0 74.6 jit_solution(11990841463723745643)
XLA Ops:
  0.6 72.0 %shard_map.131 = (bf16[256,768]{1,0:T(8,128)(2,1)}, bf16[32,4096]{1,0:T(8,128)(2,1)}) custom-call(bf16[32,4096]{1,0:T(8,128)(2,1)} %tokens_hbm.1, f32[1,4096]{1,0:T(1,128)} %bitcast.6, bf16[1,4096,768]{2,1,0:T(8,128)(2,1)} %gate_hbm.1, bf16[1,4096,768]{2,1,0:T(8,128)(2,1)} %up_hbm.1, s32[8,32]{1,0:T(8,128)} %bitcast.7, f32[8,32]{1,0:T(8,128)} %bitcast.8, ...), custom_call_target="tpu_custom_call" | custom-call | flops 6442450944 | bytes 12582912 | tf_op jit(solution)/shard_map/pallas_call | solution.py:598
  72.7 1.9 %shard_map.132 = (bf16[256,768]{1,0:T(8,128)(2,1)}, bf16[32,4096]{1,0:T(8,128)(2,1)}) custom-call(bf16[256,768]{1,0:T(8,128)(2,1)} %get-tuple-element.6.terms_in, bf16[32,4096]{1,0:T(8,128)(2,1)} %get-tuple-element.7.attended_in), custom_call_target="tpu_custom_call" | custom-call | tf_op jit(solution)/shard_map/pallas_call | solution.py:678
